TPU v7x, 32 devices: a whole 2x2x4 slice. The times are simulated.
32 devices in a mesh: groups: 2 (over x), rows: 16 (over z, y, core).
Axes of the slice: x: 2, y: 2, z: 4, core: 2. Of those that a mesh axis runs over, the one named last changes fastest.
Arguments:
- a_blocks: bfloat16 [256, 8, 256, 256], P(('groups', 'rows')), parts along dimension 0, may hold values from -8 to 8
- basis_in: bfloat16 [65536, 128], P(('groups', 'rows')), parts along dimension 0, may hold values from -5 to 5
- pattern: int32 [256, 8], P(('groups', 'rows')), parts along dimension 0, may hold values from 0 to 127, as said below
Outputs:
- basis_out: float32 [65536, 128], P(('groups', 'rows')), parts along dimension 0
- factor: float32 [256, 128], P('groups'), parts along dimension 0
There are 2 independent parts, one for each index of `groups`. A program takes and returns all parts, laid end to end along the dimension named above; each array names one. Nothing has to cross between parts.
Inputs may be any that keep to these rules, and one draw needn't show every extreme that they name: `pattern`: the 64 entries of the block rows of one device name blocks of at most 15 other devices; those naming blocks of any one other device number at most 5 and name at most 1 distinct blocks; all three bounds are reached in every draw. The entries of one block row that name blocks of other devices are distinct.
All inputs are finite; a program needn't handle non-finite values.
Results may differ from a plain program's by a relative error of at most 0.0003.
Values may be sent and summed in bfloat16 or wider, within the bound.
A program may use at most 128 MiB of HBM per device.

v0:
```python
import jax
import jax.numpy as jnp
from jax import lax
from jax.sharding import PartitionSpec as P


def upper_factor_of(matrix):
    return jnp.linalg.cholesky(matrix).T


def shards(a_blocks, basis_in, pattern):
    rank_count = lax.axis_size("rows")
    my_index = lax.axis_index("rows")
    block_rows, slot_count, block_size, unused = a_blocks.shape
    columns = basis_in.shape[1]
    own_blocks = basis_in.reshape(block_rows, block_size, columns)
    ref_count = block_rows * slot_count
    my_cols = pattern.reshape(ref_count)
    my_owner = my_cols // block_rows
    my_local = my_cols - my_owner * block_rows
    remote = my_owner != my_index
    every = lax.all_gather(pattern, "rows", axis=0, tiled=True).reshape(rank_count, ref_count)
    their_owner = every // block_rows
    their_local = every - their_owner * block_rows
    readers = jnp.arange(rank_count, dtype=jnp.int32)
    block_ids = jnp.arange(block_rows, dtype=jnp.int32)
    wanted = (their_owner == my_index) & (readers[:, None] != my_index)
    owners_hot = (my_owner[:, None] == readers[None, :]) & remote[:, None]
    owner_slots = min(ref_count - 1, rank_count - 1)
    slot_depth = (ref_count + owner_slots - 1) // owner_slots
    wanted_int = wanted.astype(jnp.int32)
    rank_in = jnp.cumsum(wanted_int, axis=1) - wanted_int
    by_slot = wanted[:, :, None] & (
        rank_in[:, :, None] == jnp.arange(slot_depth, dtype=jnp.int32)[None, None, :]
    )
    by_block = their_local[:, :, None] == block_ids[None, None, :]
    selection = jnp.einsum(
        "erk,erb->ekb",
        by_slot.astype(jnp.bfloat16),
        by_block.astype(jnp.bfloat16),
        preferred_element_type=jnp.float32,
    ).astype(jnp.bfloat16)
    outgoing = jnp.einsum(
        "ekb,bij->ekij", selection, own_blocks, preferred_element_type=jnp.float32
    ).astype(jnp.bfloat16)
    incoming = lax.all_to_all(outgoing, "rows", split_axis=0, concat_axis=0, tiled=True)
    hot_int = owners_hot.astype(jnp.int32)
    mine_rank = jnp.cumsum(hot_int, axis=0) - hot_int
    slot_index = jnp.sum(mine_rank * hot_int, axis=1)
    far_index = jnp.where(remote, my_owner * slot_depth + slot_index, 0)
    far_part = jnp.take(
        incoming.reshape(rank_count * slot_depth, block_size, columns), far_index, axis=0
    )
    local_part = jnp.take(own_blocks, my_local, axis=0)
    operand = jnp.where(remote[:, None, None], far_part, local_part).reshape(
        block_rows, slot_count, block_size, columns
    )
    product = jnp.einsum("rsij,rsjk->rik", a_blocks, operand, preferred_element_type=jnp.float32)
    image = product.reshape(block_rows * block_size, columns)
    node_count = rank_count * block_rows * block_size
    gram_local = jnp.einsum("nk,nl->kl", image, image, precision=lax.Precision.HIGHEST)
    gram = lax.psum(gram_local, "rows")
    factor = upper_factor_of(gram / node_count)
    basis_out = jax.scipy.linalg.solve_triangular(factor.T, image.T, lower=True).T
    return (basis_out, factor)


def solution(mesh):
    placed = (
        P(("groups", "rows"), None, None, None),
        P(("groups", "rows"), None),
        P(("groups", "rows"), None),
    )
    return jax.shard_map(
        shards,
        mesh=mesh,
        in_specs=placed,
        out_specs=(P(("groups", "rows"), None), P("groups", None)),
        check_vma=False,
    )
```

profile of v0, /device:TPU:0, one launch (start us, length us, event | category | flops | bytes accessed | tf_op | source)
XLA Modules:
  0.0 298.5 jit_solution(1078787044356833225)
XLA Ops:
  7.2 23.5 %all_gather.3 = s32[128,8]{1,0:T(8,128)S(1)} all-gather(s32[8,8]{1,0:T(8,128)} %param.5), channel_id=1, replica_groups=mesh['groups'=2,'rows'=16] {'rows'}, dimensions={0}, use_global_device_ids=true | all-gather | bytes 4352 | tf_op jit(solution)/shard_map/all_gather | solution.py:22
  30.7 0.1 reshape.362
  30.8 0.1 fusion.33
  30.9 0.2 reduce_window_sum.23
  31.1 0.1 fusion.11
  31.2 2.5 convolution_convert_fusion
  33.8 3.7 %copy.22 = bf16[16,5,256,128]{3,2,1,0:T(8,128)(2,1)} copy(bf16[16,5,256,128]{3,0,2,1:T(8,128)(2,1)S(1)} %convolution_convert_fusion) | data formatting | bytes 10485760 | tf_op jit(solution)/shard_map/convert_element_type | solution.py:45
  37.5 4.7 %all-to-all-start = ((bf16[16,5,256,128]{3,2,1,0:T(8,128)(2,1)}), bf16[16,5,256,128]{3,2,1,0:T(8,128)(2,1)}, u32[]{:S(2)}, u32[]{:S(2)}) async-start(bf16[16,5,256,128]{3,2,1,0:T(8,128)(2,1)} %copy.22), calls=%async_computation | async-start | bytes 10485760 | tf_op jit(solution)/shard_map/all_to_all | solution.py:46
  42.3 0.1 reshape.361
  42.4 0.1 reshape.365
  42.5 0.1 fusion.23
  42.5 0.1 reduce_window_sum.22
  42.6 0.2 select_reduce_fusion.1
  42.8 0.1 reduce_sum.14
  43.0 3.1 %gather_fusion.1 = bf16[64,256,128]{2,1,0:T(8,128)(2,1)} fusion(bf16[8,256,128]{2,1,0:T(8,128)(2,1)S(1)} %bitcast.43, s32[1024]{0:T(1024)S(1)} %pad_clamp_fusion), kind=kCustom, calls=%fused_computation.1 | custom fusion | bytes 8388864 | tf_op jit(solution)/shard_map/jit(_take)/gather | solution.py:54
  46.0 6.4 %copy.24 = bf16[64,256,128]{1,2,0:T(8,128)(2,1)} copy(bf16[64,256,128]{2,1,0:T(8,128)(2,1)} %gather_fusion.1) | data formatting | bytes 8388608 | tf_op jit(solution)/shard_map/jit(_take)/gather | solution.py:54
  52.4 85.7 %all-to-all-done = bf16[16,5,256,128]{3,2,1,0:T(8,128)(2,1)} async-done(((bf16[16,5,256,128]{3,2,1,0:T(8,128)(2,1)}), bf16[16,5,256,128]{3,2,1,0:T(8,128)(2,1)}, u32[]{:S(2)}, u32[]{:S(2)}) %all-to-all-start) | async-done | bytes 5242912 | tf_op jit(solution)/shard_map/all_to_all | solution.py:46
  138.1 5.6 %gather_fusion = bf16[64,256,128]{2,1,0:T(8,128)(2,1)} fusion(bf16[80,256,128]{2,1,0:T(8,128)(2,1)} %bitcast.3, s32[1024]{0:T(1024)S(1)} %pad_clamp_fusion.1), kind=kCustom, calls=%fused_computation | custom fusion | bytes 8388864 | tf_op jit(solution)/shard_map/jit(_take)/gather | solution.py:51
  143.7 6.4 %copy.23 = bf16[8,8,256,128]{2,3,1,0:T(8,128)(2,1)} copy(bf16[8,8,256,128]{3,2,1,0:T(8,128)(2,1)} %bitcast.44) | data formatting | bytes 8388608 | tf_op jit(solution)/shard_map/jit(_take)/gather | solution.py:51
  150.1 8.7 %fusion.8 = f32[8,256,128]{1,2,0:T(8,128)S(1)} fusion(bf16[8,8,256,256]{3,2,1,0:T(8,128)(2,1)} %param.3, bf16[8,8,256,128]{2,3,1,0:T(8,128)(2,1)} %bitcast.45, bf16[8,8,256,128]{2,3,1,0:T(8,128)(2,1)} %copy.23, pred[8,8]{1,0:T(8,128)(4,1)S(1)} %get-tuple-element.17, pred[8,8]{1,0:T(8,128)(4,1)S(1)} %get-tuple-element.18, pred[8,8]{1,0:T(8,128)(4,1)S(1)} %get-tuple-element.16), kind=kOutput, calls=%fused_computation.11 | convolution fusion | flops 1080033280 | bytes 17825984 | tf_op jit(solution)/shard_map/rsij,rsjk->rik/dot_general | solution.py:58
  158.9 1.6 convolution_bitcast_fusion
  160.5 0.3 copy.25
  160.8 103.4 %all-reduce.2.cloned.1.call-done = f32[128,128]{0,1:T(8,128)} async-done(((f32[128,128]{0,1:T(8,128)}), f32[128,128]{0,1:T(8,128)}) %all-reduce.2.cloned.1.call-update) | async-done | bytes 65552 | tf_op jit(solution)/shard_map/psum | solution.py:62
  264.3 0.8 broadcast_multiply_fusion
  265.1 0.1 copy.28
  265.2 0.9 fusion.16
  266.1 11.7 %cholesky.16 = f32[128,128]{1,0:T(8,128)S(1)} custom-call(f32[128,128]{1,0:T(8,128)S(1)} %fusion.16), custom_call_target="Cholesky" | custom-call | tf_op jit(solution)/shard_map/jit(cholesky)/cholesky | solution.py:8
  277.8 0.6 compare_reduce_fusion
  278.5 0.7 fusion.19
  279.1 9.8 %custom-call.7 = f32[1,128,128]{1,2,0:T(8,128)S(1)} custom-call(f32[1,128,128]{2,1,0:T(8,128)S(1)} %get-tuple-element.15), custom_call_target="InvertDiagBlocksLowerTriangular" | custom-call | tf_op jit(solution)/shard_map/jit(_solve_triangular)/triangular_solve | solution.py:64
  288.9 0.7 copy.29
  289.7 1.9 fusion.14
  (15 shorter events, 0.2 us)
Async XLA Ops:
  37.5 4.8 %copy-start.1 = (s32[8,8]{1,0:T(8,128)S(1)}, s32[8,8]{1,0:T(8,128)}, u32[]{:S(2)}) copy-start(s32[8,8]{1,0:T(8,128)} %param.5) | copy-start | bytes 772
  37.5 5.5 %copy-start = (bf16[2048,128]{1,0:T(8,128)(2,1)S(1)}, bf16[2048,128]{1,0:T(8,128)(2,1)}, u32[]{:S(2)}) copy-start(bf16[2048,128]{1,0:T(8,128)(2,1)} %param.4) | copy-start | bytes 1572868
  37.5 100.6 %all-to-all-start = ((bf16[16,5,256,128]{3,2,1,0:T(8,128)(2,1)}), bf16[16,5,256,128]{3,2,1,0:T(8,128)(2,1)}, u32[]{:S(2)}, u32[]{:S(2)}) async-start(bf16[16,5,256,128]{3,2,1,0:T(8,128)(2,1)} %copy.22), calls=%async_computation | async-start | bytes 10485760 | tf_op jit(solution)/shard_map/all_to_all | solution.py:46
  42.2 222.1 %all-reduce.2.cloned.1.call-start = ((), (), s32[]{:S(2)}) async-start(), calls=%async_computation.1 | async-start | bytes 131072 | tf_op jit(solution)/shard_map/psum | solution.py:62
Sparse Core Ops, SparseCore 0:
  160.6 103.6 all-reduce.1
where the time goes:
time: 300 us; the launch traced here: 298 us
  waiting for transfers between devices  189 us (63%)
  local copies, waits for them, and re-layouts  26.6 us (9%)
  other arithmetic  25.3 us (8%)
  blocking collectives  23.5 us (8%)
  matrix products  15 us (5%)
  between operations  14.2 us (5%)
  starting transfers between devices  4.74 us (2%)
    psum x1, waiting for transfers between devices, shards(): gram = lax.psum(gram_local, 'rows')  103 us
    all_to_all x1, waiting for transfers between devices, shards(): lax.all_to_all(outgoing, 'rows', split_axis=0, concat_axis=0, tiled=True)  85.7 us
    all_gather x1, blocking collectives, shards(): lax.all_gather(pattern, 'rows', axis=0, tiled=True)  23.5 us
    another operation x3, other arithmetic, upper_factor_of(): return jnp.linalg.cholesky(matrix).T  12.4 us
    gather x2, local copies, waits for them, and re-layouts, shards(): jnp.take(incoming.reshape(rank_count * slot_depth, block_size, columns),...  12 us
    another operation x1, other arithmetic, shards(): jax.scipy.linalg.solve_triangular(factor.T, image.T, lower=True)  9.81 us
    gather x2, local copies, waits for them, and re-layouts, shards(): local_part = jnp.take(own_blocks, my_local, axis=0)  9.43 us
    dot_general x1, matrix products, shards(): jnp.einsum('rsij,rsjk->rik', a_blocks, operand, preferred_element_type=jn...  8.75 us
  transfers between devices with their start and end apart: 2, of which 2 were waited for; matrix products, arithmetic and copies ran while one was open for 3% of the time, Pallas kernels for 0%

commit v1 on v0

v1 whole, which is shorter than its diff:
```python
import functools
import jax
import jax.numpy as jnp
from jax import lax
from jax.experimental import pallas as pl
from jax.experimental.pallas import tpu as pltpu
from jax.sharding import PartitionSpec as P

MESH = pl.DeviceIdType.MESH
F32 = jnp.float32
BF16 = jnp.bfloat16


def split(x):
    hi = x.astype(BF16)
    lo = (x - hi.astype(F32)).astype(BF16)
    return hi, lo


def product_kernel(
    n, m, a_hbm, basis, pat_v, pat_s, image_hbm, gram_out,
    a_vm, req_out, req_in, out_buf, land, stage, acc, part, gram_in, chunk,
    slot_s, index_s,
    a_sem, image_sem, req_send, req_recv, dat_send, dat_recv, rs_send, rs_recv, ag_send, ag_recv,
):
    me = lax.axis_index("rows")
    rows, slots = pat_s.shape
    cols = part.shape[1]
    share = chunk.shape[0]

    def offset(k):
        return n // 2 + ((k + 1) // 2) * (1 - 2 * (k % 2))

    def remote(src, dst, send, recv, target):
        return pltpu.make_async_remote_copy(
            src_ref=src, dst_ref=dst, send_sem=send, recv_sem=recv,
            device_id={"rows": target}, device_id_type=MESH,
        )

    barrier = pltpu.get_barrier_semaphore()

    @pl.loop(0, n - 1)
    def _(k):
        pl.semaphore_signal(
            barrier, inc=1, device_id={"rows": (me + k + 1) % n}, device_id_type=MESH
        )

    a_copy = pltpu.make_async_copy(a_hbm, a_vm, a_sem)
    a_copy.start()
    pattern = pat_v[...][None]
    owner_ids = lax.broadcasted_iota(jnp.int32, (n, rows, slots), 0)
    local = pattern - owner_ids * rows
    named = jnp.where((local >= 0) & (local < rows), local, 0)
    asked = jnp.max(jnp.max(named, axis=2, keepdims=True), axis=1, keepdims=True)
    req_out[...] = jnp.broadcast_to(asked, req_out.shape)
    pl.semaphore_wait(barrier, n - 1)

    @pl.loop(0, n - 1)
    def _(k):
        target = (me + n - offset(k)) % n
        remote(
            req_out.at[target], req_in.at[me], req_send.at[target], req_recv.at[me], target
        ).start()

    @pl.loop(0, n - 1)
    def _(k):
        target = (me + offset(k)) % n
        remote(
            req_out.at[target], req_in.at[target], req_send.at[target], req_recv.at[target], target
        ).wait_recv()
        wanted = req_in[target][0, 0]
        out_buf[target] = basis[wanted]
        remote(
            out_buf.at[target], land.at[me], dat_send.at[target], dat_recv.at[me], target
        ).start()

    for b in range(rows):
        stage[b] = basis[b]

    @pl.loop(0, rows)
    def _(r):
        keys = []
        places = []
        for s in range(slots):
            col = pat_s[r, s]
            owner = col // rows
            delta = (me - owner + n) % n - n // 2
            rank = jnp.where(delta > 0, 2 * delta, -2 * delta - 1)
            rank = jnp.where(delta == 0, 0, rank)
            rank = jnp.where(owner == me, -1, rank)
            keys.append(rank * slots + s)
            places.append(jnp.where(owner == me, col - owner * rows, rows + owner))
        position = []
        for s in range(slots):
            count = 0
            for t in range(slots):
                if t != s:
                    count = count + jnp.where(keys[t] < keys[s], 1, 0)
            position.append(count)
        for k in range(slots):
            slot = 0
            place = 0
            for s in range(slots):
                slot = jnp.where(position[s] == k, s, slot)
                place = jnp.where(position[s] == k, places[s], place)
            slot_s[r, k] = slot
            index_s[r, k] = place

    def arrive(k):
        source = (me + n - offset(k)) % n
        remote(
            out_buf.at[source], land.at[source], dat_send.at[source], dat_recv.at[source], source
        ).wait_recv()
        stage[rows + source] = land[source]

    @pl.loop(0, n - 1 - slots)
    def _(k):
        arrive(k)

    a_copy.wait()

    for k in range(slots):
        arrive(n - 1 - slots + k)

        @pl.loop(0, rows)
        def _(r):
            term = jnp.dot(
                a_vm[r, slot_s[r, k]], stage[index_s[r, k]], preferred_element_type=F32
            )
            if k == 0:
                acc[r] = term
            else:
                acc[r] += term

    image_copy = pltpu.make_async_copy(acc, image_hbm, image_sem)
    image_copy.start()

    total = jnp.zeros((cols, 2 * cols), F32)
    for r in range(rows):
        hi, lo = split(acc[r])
        total = total + lax.dot_general(
            hi, jnp.concatenate([hi, lo], axis=1), (((0,), (0,)), ((), ())),
            preferred_element_type=F32,
        )
    cross = total[:, cols:]
    part[...] = total[:, :cols] + cross + cross.T

    @pl.loop(0, m)
    def _(t):
        @pl.when(t != me)
        def _():
            remote(
                part.at[pl.ds(t * share, share)], gram_in.at[me], rs_send.at[t], rs_recv.at[me], t
            ).start()

    @pl.when(me < m)
    def _():
        gram_in[me] = part[pl.ds(pl.multiple_of(me * share, share), share), :]

        @pl.loop(0, n - 1)
        def _(k):
            source = (me + k + 1) % n
            remote(
                part.at[pl.ds(0, share)], gram_in.at[source], rs_send.at[0], rs_recv.at[source], source
            ).wait_recv()

        chunk[...] = jnp.sum(gram_in[...], axis=0)

        @pl.loop(0, n - 1)
        def _(k):
            target = (me + k + 1) % n
            remote(
                chunk, gram_out.at[pl.ds(me * share, share)], ag_send.at[target], ag_recv.at[me], target
            ).start()

        gram_out[pl.ds(pl.multiple_of(me * share, share), share), :] = chunk[...]

    @pl.loop(0, m)
    def _(t):
        @pl.when(t != me)
        def _():
            remote(
                chunk, gram_out.at[pl.ds(t * share, share)], ag_send.at[t], ag_recv.at[t], t
            ).wait_recv()
            remote(
                part.at[pl.ds(t * share, share)], gram_in.at[me], rs_send.at[t], rs_recv.at[me], t
            ).wait_send()

    @pl.when(me < m)
    def _():
        @pl.loop(0, n - 1)
        def _(k):
            target = (me + k + 1) % n
            remote(
                chunk, gram_out.at[pl.ds(me * share, share)], ag_send.at[target], ag_recv.at[me], target
            ).wait_send()

    @pl.loop(0, n - 1)
    def _(k):
        target = (me + k + 1) % n
        remote(
            req_out.at[target], req_in.at[me], req_send.at[target], req_recv.at[me], target
        ).wait_send()
        remote(
            out_buf.at[target], land.at[me], dat_send.at[target], dat_recv.at[me], target
        ).wait_send()

    image_copy.wait()


def product_and_gram(a_blocks, own_blocks, pattern):
    n = lax.axis_size("rows")
    rows, slots, size, unused = a_blocks.shape
    cols = own_blocks.shape[2]
    share = 8
    m = cols // share
    assert n >= m and n > slots
    vmem = pl.BlockSpec(memory_space=pltpu.VMEM)
    dma = pltpu.SemaphoreType.DMA
    return pl.pallas_call(
        functools.partial(product_kernel, n, m),
        out_shape=(
            jax.ShapeDtypeStruct((rows, size, cols), F32),
            jax.ShapeDtypeStruct((cols, cols), F32),
        ),
        in_specs=[
            pl.BlockSpec(memory_space=pl.ANY), vmem, vmem, pl.BlockSpec(memory_space=pltpu.SMEM),
        ],
        out_specs=(pl.BlockSpec(memory_space=pl.ANY), vmem),
        scratch_shapes=[
            pltpu.VMEM(a_blocks.shape, BF16),
            pltpu.VMEM((n, 1, 128), jnp.int32),
            pltpu.VMEM((n, 1, 128), jnp.int32),
            pltpu.VMEM((n, size, cols), BF16),
            pltpu.VMEM((n, size, cols), BF16),
            pltpu.VMEM((rows + n, size, cols), BF16),
            pltpu.VMEM((rows, size, cols), F32),
            pltpu.VMEM((cols, cols), F32),
            pltpu.VMEM((n, share, cols), F32),
            pltpu.VMEM((share, cols), F32),
            pltpu.SMEM((rows, slots), jnp.int32),
            pltpu.SMEM((rows, slots), jnp.int32),
            dma, dma,
            dma((n,)), dma((n,)), dma((n,)), dma((n,)),
            dma((n,)), dma((n,)), dma((n,)), dma((n,)),
        ],
        compiler_params=pltpu.CompilerParams(
            collective_id=0, has_side_effects=True, vmem_limit_bytes=52 * 1024 * 1024
        ),
        name="product_and_gram",
    )(a_blocks, own_blocks, pattern, pattern)


def shards(a_blocks, basis_in, pattern):
    n = lax.axis_size("rows")
    rows, slots, size, unused = a_blocks.shape
    cols = basis_in.shape[1]
    image, gram = product_and_gram(a_blocks, basis_in.reshape(rows, size, cols), pattern)
    image = image.reshape(rows * size, cols)
    factor = jnp.linalg.cholesky(gram / (n * rows * size)).T
    basis_out = jax.scipy.linalg.solve_triangular(factor.T, image.T, lower=True).T
    return (basis_out, factor)


def solution(mesh):
    placed = (
        P(("groups", "rows"), None, None, None),
        P(("groups", "rows"), None),
        P(("groups", "rows"), None),
    )
    return jax.shard_map(
        shards,
        mesh=mesh,
        in_specs=placed,
        out_specs=(P(("groups", "rows"), None), P("groups", None)),
        check_vma=False,
    )
```

time: 300 us -> 81.2 us (0.27)
  waiting for transfers between devices: 189 us -> 0 us
  Pallas kernels: 0 us -> 52.8 us
  local copies, waits for them, and re-layouts: 26.6 us -> 2.63 us
  blocking collectives: 23.5 us -> 0 us
  between operations: 14.2 us -> 0.69 us
  matrix products: 15 us -> 1.94 us
  starting transfers between devices: 4.74 us -> 0 us
    psum x1 -> x0, waiting for transfers between devices: 103 us -> none  [shards(): gram = lax.psum(gram_local, 'rows')]
    all_to_all x1 -> x0, waiting for transfers between devices: 85.7 us -> none  [shards(): lax.all_to_all(outgoing, 'rows', split_axis=0, concat_axis=0, tiled=True)]
    pallas_call x0 -> x1, Pallas kernels: none -> 52.8 us  [product_and_gram(): pl.pallas_call(functools.partial(product_kernel, n, m), out_shape=(jax.Sh...]
    all_gather x1 -> x0, blocking collectives: 23.5 us -> none  [shards(): lax.all_gather(pattern, 'rows', axis=0, tiled=True)]
    gather x4 -> x0, local copies, waits for them, and re-layouts: 21.5 us -> none  [the longest x2 12 us: shards(): jnp.take(incoming.reshape(rank_count * slot_depth, block_size, columns),...]
    dot_general x4 -> x0, matrix products: 13.1 us -> none  [the longest x1 8.75 us: shards(): jnp.einsum('rsij,rsjk->rik', a_blocks, operand, preferred_element_type=jn...]
    all_to_all x1 -> x0, starting transfers between devices: 4.7 us -> none  [shards(): lax.all_to_all(outgoing, 'rows', split_axis=0, concat_axis=0, tiled=True)]
    convert_element_type x1 -> x0, local copies, waits for them, and re-layouts: 3.71 us -> none  [shards(): outgoing = jnp.einsum('ekb,bij->ekij', selection, own_blocks, preferred_e...]
  transfers between devices with their start and end apart: 2 -> 0, of which waited for: 2 -> 0; matrix products, arithmetic and copies ran while one was open for 3% -> 0% of each run, Pallas kernels for 0% -> 0%
where the time goes in v1:
time: 81.2 us; the launch traced here: 81 us
  Pallas kernels  52.8 us (65%)
  other arithmetic  22.9 us (28%)
  local copies, waits for them, and re-layouts  2.63 us (3%)
  matrix products  1.94 us (2%)
    pallas_call x1, Pallas kernels, product_and_gram(): pl.pallas_call(functools.partial(product_kernel, n, m), out_shape=(jax.Sh...  52.8 us
    another operation x3, other arithmetic, shards(): factor = jnp.linalg.cholesky(gram / (n * rows * size)).T  12.4 us
    another operation x1, other arithmetic, shards(): jax.scipy.linalg.solve_triangular(factor.T, image.T, lower=True)  9.81 us
    unnamed x5, local copies, waits for them, and re-layouts  2.45 us
    another operation x1, matrix products, shards(): jax.scipy.linalg.solve_triangular(factor.T, image.T, lower=True)  1.94 us

profile of v1, /device:TPU:0, one launch (start us, length us, event | category | flops | bytes accessed | tf_op | source)
XLA Modules:
  0.0 81.0 jit_solution(14497002565979008322)
XLA Ops:
  0.6 0.0 copy-start
  0.6 1.0 %copy-done = bf16[2048,128]{1,0:T(8,128)(2,1)S(1)} copy-done((bf16[2048,128]{1,0:T(8,128)(2,1)S(1)}, bf16[2048,128]{1,0:T(8,128)(2,1)}, u32[]{:S(2)}) %copy-start) | copy-done | bytes 524312
  1.7 0.0 copy-start.1
  1.7 0.7 copy-done.1
  2.4 52.8 %product_and_gram.1 = (f32[8,256,128]{2,1,0:T(8,128)S(1)}, f32[128,128]{1,0:T(8,128)S(1)}) custom-call(bf16[8,8,256,256]{3,2,1,0:T(8,128)(2,1)} %a_hbm.1, bf16[8,256,128]{2,1,0:T(8,128)(2,1)S(1)} %bitcast.15, s32[8,8]{1,0:T(8,128)S(1)} %copy-done.1, s32[8,8]{1,0:T(8,128)S(1)} %copy-done.1), custom_call_target="tpu_custom_call" | custom-call | tf_op jit(solution)/shard_map/product_and_gram/pallas_call | solution.py:220
  55.2 0.1 copy.5
  55.3 0.1 copy.6
  55.4 11.7 %cholesky.16 = f32[128,128]{1,0:T(8,128)S(1)} custom-call(f32[128,128]{1,0:T(8,128)S(1)} %fusion.2), custom_call_target="Cholesky" | custom-call | tf_op jit(solution)/shard_map/jit(cholesky)/cholesky | solution.py:260
  67.2 0.6 compare_reduce_fusion
  67.8 0.7 fusion.3
  68.5 0.7 copy.7
  69.2 9.8 %custom-call.7 = f32[1,128,128]{1,2,0:T(8,128)S(1)} custom-call(f32[1,128,128]{2,1,0:T(8,128)S(1)} %get-tuple-element.9), custom_call_target="InvertDiagBlocksLowerTriangular" | custom-call | tf_op jit(solution)/shard_map/jit(_solve_triangular)/triangular_solve | solution.py:261
  79.0 1.9 %fusion = f32[2048,128]{1,0:T(8,128)} fusion(f32[2048,128]{1,0:T(8,128)S(1)} %bitcast.14, f32[1,128,128]{1,2,0:T(8,128)S(1)} %custom-call.7), kind=kOutput, calls=%fused_computation | convolution fusion | flops 402653184 | bytes 2162688 | tf_op jit(solution)/shard_map/jit(_solve_triangular)/triangular_solve | solution.py:261
  (3 shorter events, 0.1 us)
Async XLA Ops:
  0.6 1.0 %copy-start = (bf16[2048,128]{1,0:T(8,128)(2,1)S(1)}, bf16[2048,128]{1,0:T(8,128)(2,1)}, u32[]{:S(2)}) copy-start(bf16[2048,128]{1,0:T(8,128)(2,1)} %param.4) | copy-start | bytes 1572868
  1.7 0.7 copy-start.1

commit v2 on v1

--- a/solution.py
+++ b/solution.py
@@ -9,6 +9,7 @@
 MESH = pl.DeviceIdType.MESH
 F32 = jnp.float32
 BF16 = jnp.bfloat16
+STEP = 16
 
 
 def split(x):
@@ -28,8 +29,14 @@
     cols = part.shape[1]
     share = chunk.shape[0]
 
-    def offset(k):
-        return n // 2 + ((k + 1) // 2) * (1 - 2 * (k % 2))
+    def partner(k):
+        d = k + 1
+        other = me + d
+        bit = 1
+        while bit < n:
+            other = other - 2 * bit * ((me // bit) % 2) * ((d // bit) % 2)
+            bit *= 2
+        return other
 
     def remote(src, dst, send, recv, target):
         return pltpu.make_async_remote_copy(
@@ -57,14 +64,14 @@
 
     @pl.loop(0, n - 1)
     def _(k):
-        target = (me + n - offset(k)) % n
+        target = partner(k)
         remote(
             req_out.at[target], req_in.at[me], req_send.at[target], req_recv.at[me], target
         ).start()
 
     @pl.loop(0, n - 1)
     def _(k):
-        target = (me + offset(k)) % n
+        target = partner(k)
         remote(
             req_out.at[target], req_in.at[target], req_send.at[target], req_recv.at[target], target
         ).wait_recv()
@@ -84,10 +91,7 @@
         for s in range(slots):
             col = pat_s[r, s]
             owner = col // rows
-            delta = (me - owner + n) % n - n // 2
-            rank = jnp.where(delta > 0, 2 * delta, -2 * delta - 1)
-            rank = jnp.where(delta == 0, 0, rank)
-            rank = jnp.where(owner == me, -1, rank)
+            rank = jnp.bitwise_xor(owner, me)
             keys.append(rank * slots + s)
             places.append(jnp.where(owner == me, col - owner * rows, rows + owner))
         position = []
@@ -107,7 +111,7 @@
             index_s[r, k] = place
 
     def arrive(k):
-        source = (me + n - offset(k)) % n
+        source = partner(k)
         remote(
             out_buf.at[source], land.at[source], dat_send.at[source], dat_recv.at[source], source
         ).wait_recv()
@@ -214,7 +218,7 @@
     cols = own_blocks.shape[2]
     share = 8
     m = cols // share
-    assert n >= m and n > slots
+    assert n >= m and n > slots and n & (n - 1) == 0
     vmem = pl.BlockSpec(memory_space=pltpu.VMEM)
     dma = pltpu.SemaphoreType.DMA
     return pl.pallas_call(
@@ -251,15 +255,123 @@
     )(a_blocks, own_blocks, pattern, pattern)
 
 
+def lanes(x, width):
+    return jnp.broadcast_to(x, (x.shape[0], width))
+
+
+def sublanes(x, i):
+    return jnp.broadcast_to(x[i:i + 1], x.shape)
+
+
+def three(x):
+    high = x.astype(BF16).astype(F32)
+    rest = x - high
+    middle = rest.astype(BF16).astype(F32)
+    return high, middle, rest - middle
+
+
+def factor_kernel(scale, step, gram, image_hbm, basis_hbm, factor, image, result, in_sem, out_sem):
+    cols = gram.shape[0]
+    chunks, size, unused = image.shape
+    image_copy = pltpu.make_async_copy(image_hbm, image, in_sem)
+    image_copy.start()
+    down = lax.broadcasted_iota(jnp.int32, (cols, cols), 0)
+    across = lax.broadcasted_iota(jnp.int32, (cols, cols), 1)
+    rest = jnp.concatenate([gram[...] * scale, jnp.where(down == across, 1.0, 0.0)], axis=1)
+    halves = step // 8
+    sub = lax.broadcasted_iota(jnp.int32, (8, cols), 0)
+    uppers = []
+    lowers = []
+    for start in range(0, cols, step):
+        panel = [rest[8 * h:8 * h + 8] for h in range(halves)]
+        column = [
+            [lanes(panel[h][:, start + l:start + l + 1], cols) for h in range(halves)]
+            for l in range(step)
+        ]
+        left = [p[:, :cols] for p in panel]
+        right = [p[:, cols:] for p in panel]
+        pivots = [jnp.ones((8, cols), F32) for h in range(halves)]
+        for k in range(step):
+            h0, i0 = divmod(k, 8)
+            pivot = sublanes(column[k][h0], i0)
+            pivots[h0] = jnp.where(sub == i0, pivot, pivots[h0])
+            inverse = 1.0 / pivot
+            below = [
+                jnp.where(sub > i0, column[k][h], 0.0) if h == h0 else column[k][h]
+                for h in range(h0, halves)
+            ]
+            for l in range(k + 1, step):
+                weight = sublanes(column[l][h0], i0) * inverse
+                for h in range(h0, halves):
+                    column[l][h] = column[l][h] - below[h - h0] * weight
+            top_left = sublanes(left[h0], i0) * inverse
+            top_right = sublanes(right[h0], i0) * inverse
+            for h in range(h0, halves):
+                left[h] = left[h] - below[h - h0] * top_left
+                right[h] = right[h] - below[h - h0] * top_right
+        roots = [lax.rsqrt(p) for p in pivots]
+        new_left = jnp.concatenate([l * r for l, r in zip(left, roots)], axis=0)
+        new_right = jnp.concatenate([l * r for l, r in zip(right, roots)], axis=0)
+        uppers.append(new_left)
+        lowers.append(new_right)
+        if start + step < cols:
+            a1, a2, a3 = three(new_left)
+            b1, b2, b3 = three(new_right)
+            lhs = jnp.concatenate([a1, a1, a2, a2, a1, a3], axis=0).astype(BF16)
+            rhs = jnp.concatenate(
+                [
+                    jnp.concatenate([a1, a2, a1, a2, a3, a1], axis=0),
+                    jnp.concatenate([b1, b2, b1, b2, b3, b1], axis=0),
+                ],
+                axis=1,
+            ).astype(BF16)
+            change = lax.dot_general(
+                lhs, rhs, (((0,), (0,)), ((), ())), preferred_element_type=F32
+            )
+            rest = rest[step:] - change[start + step:]
+    upper = jnp.concatenate(uppers, axis=0)
+    lower = jnp.concatenate(lowers, axis=0)
+    factor[...] = jnp.where(across >= down, upper, 0.0)
+    high, low = split(lower)
+    both = jnp.concatenate([high, high], axis=1)
+    image_copy.wait()
+    turned = (((1,), (1,)), ((), ()))
+    for c in range(chunks):
+        x_high, x_low = split(image[c])
+        result[c] = lax.dot_general(
+            jnp.concatenate([x_high, x_low], axis=1), both, turned, preferred_element_type=F32
+        ) + lax.dot_general(x_high, low, turned, preferred_element_type=F32)
+        pltpu.make_async_copy(result.at[c], basis_hbm.at[c], out_sem.at[c]).start()
+    for c in range(chunks):
+        pltpu.make_async_copy(result.at[c], basis_hbm.at[c], out_sem.at[c]).wait()
+
+
+def factor_and_basis(gram, image, nodes):
+    vmem = pl.BlockSpec(memory_space=pltpu.VMEM)
+    dma = pltpu.SemaphoreType.DMA
+    return pl.pallas_call(
+        functools.partial(factor_kernel, 1.0 / nodes, STEP),
+        out_shape=(
+            jax.ShapeDtypeStruct(image.shape, F32),
+            jax.ShapeDtypeStruct(gram.shape, F32),
+        ),
+        in_specs=[vmem, pl.BlockSpec(memory_space=pl.ANY)],
+        out_specs=(pl.BlockSpec(memory_space=pl.ANY), vmem),
+        scratch_shapes=[
+            pltpu.VMEM(image.shape, F32), pltpu.VMEM(image.shape, F32), dma, dma((image.shape[0],)),
+        ],
+        compiler_params=pltpu.CompilerParams(vmem_limit_bytes=32 * 1024 * 1024),
+        name="factor_and_basis",
+    )(gram, image)
+
+
 def shards(a_blocks, basis_in, pattern):
     n = lax.axis_size("rows")
     rows, slots, size, unused = a_blocks.shape
     cols = basis_in.shape[1]
     image, gram = product_and_gram(a_blocks, basis_in.reshape(rows, size, cols), pattern)
-    image = image.reshape(rows * size, cols)
-    factor = jnp.linalg.cholesky(gram / (n * rows * size)).T
-    basis_out = jax.scipy.linalg.solve_triangular(factor.T, image.T, lower=True).T
-    return (basis_out, factor)
+    basis_out, factor = factor_and_basis(gram, image, n * rows * size)
+    return (basis_out.reshape(rows * size, cols), factor)
 
 
 def solution(mesh):

time: 81.2 us -> 55.3 us (0.68)
  other arithmetic: 22.9 us -> 0 us
  matrix products: 1.94 us -> 0 us
  local copies, waits for them, and re-layouts: 2.63 us -> 1.72 us
    another operation x4 -> x0, other arithmetic: 22.2 us -> none  [the longest x3 12.4 us: shards(): factor = jnp.linalg.cholesky(gram / (n * rows * size)).T]
    pallas_call x1, Pallas kernels: 52.8 us -> 47.2 us  [product_and_gram(): pl.pallas_call(functools.partial(product_kernel, n, m), out_shape=(jax.Sh...]
    pallas_call x0 -> x1, Pallas kernels: none -> 5.56 us  [factor_and_basis(): pl.pallas_call(functools.partial(factor_kernel, 1.0 / nodes, STEP), out_s...]
    another operation x1 -> x0, matrix products: 1.94 us -> none  [shards(): jax.scipy.linalg.solve_triangular(factor.T, image.T, lower=True)]
    unnamed x5 -> x4, local copies, waits for them, and re-layouts: 2.45 us -> 1.72 us
where the time goes in v2:
time: 55.3 us; the launch traced here: 55.1 us
  Pallas kernels  52.8 us (95%)
  local copies, waits for them, and re-layouts  1.72 us (3%)
  between operations  0.65 us (1%)
    pallas_call x1, Pallas kernels, product_and_gram(): pl.pallas_call(functools.partial(product_kernel, n, m), out_shape=(jax.Sh...  47.2 us
    pallas_call x1, Pallas kernels, factor_and_basis(): pl.pallas_call(functools.partial(factor_kernel, 1.0 / nodes, STEP), out_s...  5.56 us
    unnamed x4, local copies, waits for them, and re-layouts  1.72 us

profile of v2, /device:TPU:0, one launch (start us, length us, event | category | flops | bytes accessed | tf_op | source)
XLA Modules:
  0.0 55.1 jit_solution(1490928276113035711)
XLA Ops:
  0.6 0.0 copy-start
  0.6 1.0 %copy-done = bf16[2048,128]{1,0:T(8,128)(2,1)S(1)} copy-done((bf16[2048,128]{1,0:T(8,128)(2,1)S(1)}, bf16[2048,128]{1,0:T(8,128)(2,1)}, u32[]{:S(2)}) %copy-start) | copy-done | bytes 524312
  1.7 0.0 copy-start.1
  1.7 0.7 %copy-done.1 = s32[8,8]{1,0:T(8,128)S(1)} copy-done((s32[8,8]{1,0:T(8,128)S(1)}, s32[8,8]{1,0:T(8,128)}, u32[]{:S(2)}) %copy-start.1) | copy-done | bytes 280
  2.4 47.2 %product_and_gram.1 = (f32[8,256,128]{2,1,0:T(8,128)S(1)}, f32[128,128]{1,0:T(8,128)S(1)}) custom-call(bf16[8,8,256,256]{3,2,1,0:T(8,128)(2,1)} %a_hbm.1, bf16[8,256,128]{2,1,0:T(8,128)(2,1)S(1)} %bitcast.2, s32[8,8]{1,0:T(8,128)S(1)} %copy-done.1, s32[8,8]{1,0:T(8,128)S(1)} %copy-done.1), custom_call_target="tpu_custom_call" | custom-call | tf_op jit(solution)/shard_map/product_and_gram/pallas_call | solution.py:224
  49.6 5.6 %factor_and_basis.1 = (f32[8,256,128]{2,1,0:T(8,128)}, f32[128,128]{1,0:T(8,128)}) custom-call(f32[128,128]{1,0:T(8,128)S(1)} %get-tuple-element.6.gram, f32[8,256,128]{2,1,0:T(8,128)S(1)} %get-tuple-element.7.image_hbm), custom_call_target="tpu_custom_call" | custom-call | tf_op jit(solution)/shard_map/factor_and_basis/pallas_call | solution.py:352
Async XLA Ops:
  0.6 1.0 %copy-start = (bf16[2048,128]{1,0:T(8,128)(2,1)S(1)}, bf16[2048,128]{1,0:T(8,128)(2,1)}, u32[]{:S(2)}) copy-start(bf16[2048,128]{1,0:T(8,128)(2,1)} %param.4) | copy-start | bytes 1572868
  1.7 0.7 %copy-start.1 = (s32[8,8]{1,0:T(8,128)S(1)}, s32[8,8]{1,0:T(8,128)}, u32[]{:S(2)}) copy-start(s32[8,8]{1,0:T(8,128)} %pat_s.1) | copy-start | bytes 772

commit v3 on v2

--- a/solution.py
+++ b/solution.py
@@ -19,10 +19,10 @@
 
 
 def product_kernel(
-    n, m, a_hbm, basis, pat_v, pat_s, image_hbm, gram_out,
-    a_vm, req_out, req_in, out_buf, land, stage, acc, part, gram_in, chunk,
+    n, m, a_hbm, basis_hbm, pat_hbm, image_hbm, gram_out,
+    pat_v, pat_s, a_vm, req_out, req_in, out_buf, land, stage, acc, part, gram_in, chunk,
     slot_s, index_s,
-    a_sem, image_sem, req_send, req_recv, dat_send, dat_recv, rs_send, rs_recv, ag_send, ag_recv,
+    a_sem, basis_sem, pat_v_sem, pat_s_sem, image_sem, req_send, req_recv, dat_send, dat_recv, rs_send, rs_recv, ag_send, ag_recv,
 ):
     me = lax.axis_index("rows")
     rows, slots = pat_s.shape
@@ -44,9 +44,16 @@
             device_id={"rows": target}, device_id_type=MESH,
         )
 
+    unroll = n <= 16
+    pat_v_copy = pltpu.make_async_copy(pat_hbm, pat_v, pat_v_sem)
+    pat_v_copy.start()
+    pat_s_copy = pltpu.make_async_copy(pat_hbm, pat_s, pat_s_sem)
+    pat_s_copy.start()
+    basis_copy = pltpu.make_async_copy(basis_hbm, stage.at[pl.ds(0, rows)], basis_sem)
+    basis_copy.start()
     barrier = pltpu.get_barrier_semaphore()
 
-    @pl.loop(0, n - 1)
+    @pl.loop(0, n - 1, unroll=unroll)
     def _(k):
         pl.semaphore_signal(
             barrier, inc=1, device_id={"rows": (me + k + 1) % n}, device_id_type=MESH
@@ -54,35 +61,35 @@
 
     a_copy = pltpu.make_async_copy(a_hbm, a_vm, a_sem)
     a_copy.start()
+    pat_v_copy.wait()
     pattern = pat_v[...][None]
     owner_ids = lax.broadcasted_iota(jnp.int32, (n, rows, slots), 0)
     local = pattern - owner_ids * rows
     named = jnp.where((local >= 0) & (local < rows), local, 0)
     asked = jnp.max(jnp.max(named, axis=2, keepdims=True), axis=1, keepdims=True)
     req_out[...] = jnp.broadcast_to(asked, req_out.shape)
+    basis_copy.wait()
+    pat_s_copy.wait()
     pl.semaphore_wait(barrier, n - 1)
 
-    @pl.loop(0, n - 1)
+    @pl.loop(0, n - 1, unroll=unroll)
     def _(k):
         target = partner(k)
         remote(
             req_out.at[target], req_in.at[me], req_send.at[target], req_recv.at[me], target
         ).start()
 
-    @pl.loop(0, n - 1)
+    @pl.loop(0, n - 1, unroll=unroll)
     def _(k):
         target = partner(k)
         remote(
             req_out.at[target], req_in.at[target], req_send.at[target], req_recv.at[target], target
         ).wait_recv()
         wanted = req_in[target][0, 0]
-        out_buf[target] = basis[wanted]
+        out_buf[target] = stage[wanted]
         remote(
             out_buf.at[target], land.at[me], dat_send.at[target], dat_recv.at[me], target
         ).start()
-
-    for b in range(rows):
-        stage[b] = basis[b]
 
     @pl.loop(0, rows)
     def _(r):
@@ -126,30 +133,27 @@
     for k in range(slots):
         arrive(n - 1 - slots + k)
 
-        @pl.loop(0, rows)
-        def _(r):
+        for r in range(rows):
             term = jnp.dot(
                 a_vm[r, slot_s[r, k]], stage[index_s[r, k]], preferred_element_type=F32
             )
-            if k == 0:
-                acc[r] = term
-            else:
-                acc[r] += term
+            if k > 0:
+                term = term + acc[r]
+            acc[r] = term
+            if k == slots - 1:
+                high, low = split(term)
+                square = lax.dot_general(
+                    high, jnp.concatenate([high, low], axis=1), (((0,), (0,)), ((), ())),
+                    preferred_element_type=F32,
+                )
+                total = square if r == 0 else total + square
 
     image_copy = pltpu.make_async_copy(acc, image_hbm, image_sem)
     image_copy.start()
-
-    total = jnp.zeros((cols, 2 * cols), F32)
-    for r in range(rows):
-        hi, lo = split(acc[r])
-        total = total + lax.dot_general(
-            hi, jnp.concatenate([hi, lo], axis=1), (((0,), (0,)), ((), ())),
-            preferred_element_type=F32,
-        )
     cross = total[:, cols:]
     part[...] = total[:, :cols] + cross + cross.T
 
-    @pl.loop(0, m)
+    @pl.loop(0, m, unroll=unroll)
     def _(t):
         @pl.when(t != me)
         def _():
@@ -161,7 +165,7 @@
     def _():
         gram_in[me] = part[pl.ds(pl.multiple_of(me * share, share), share), :]
 
-        @pl.loop(0, n - 1)
+        @pl.loop(0, n - 1, unroll=unroll)
         def _(k):
             source = (me + k + 1) % n
             remote(
@@ -170,7 +174,7 @@
 
         chunk[...] = jnp.sum(gram_in[...], axis=0)
 
-        @pl.loop(0, n - 1)
+        @pl.loop(0, n - 1, unroll=unroll)
         def _(k):
             target = (me + k + 1) % n
             remote(
@@ -179,7 +183,7 @@
 
         gram_out[pl.ds(pl.multiple_of(me * share, share), share), :] = chunk[...]
 
-    @pl.loop(0, m)
+    @pl.loop(0, m, unroll=unroll)
     def _(t):
         @pl.when(t != me)
         def _():
@@ -192,14 +196,14 @@
 
     @pl.when(me < m)
     def _():
-        @pl.loop(0, n - 1)
+        @pl.loop(0, n - 1, unroll=unroll)
         def _(k):
             target = (me + k + 1) % n
             remote(
                 chunk, gram_out.at[pl.ds(me * share, share)], ag_send.at[target], ag_recv.at[me], target
             ).wait_send()
 
-    @pl.loop(0, n - 1)
+    @pl.loop(0, n - 1, unroll=unroll)
     def _(k):
         target = (me + k + 1) % n
         remote(
@@ -228,10 +232,14 @@
             jax.ShapeDtypeStruct((cols, cols), F32),
         ),
         in_specs=[
-            pl.BlockSpec(memory_space=pl.ANY), vmem, vmem, pl.BlockSpec(memory_space=pltpu.SMEM),
+            pl.BlockSpec(memory_space=pltpu.HBM),
+            pl.BlockSpec(memory_space=pltpu.HBM),
+            pl.BlockSpec(memory_space=pltpu.HBM),
         ],
         out_specs=(pl.BlockSpec(memory_space=pl.ANY), vmem),
         scratch_shapes=[
+            pltpu.VMEM((rows, slots), jnp.int32),
+            pltpu.SMEM((rows, slots), jnp.int32),
             pltpu.VMEM(a_blocks.shape, BF16),
             pltpu.VMEM((n, 1, 128), jnp.int32),
             pltpu.VMEM((n, 1, 128), jnp.int32),
@@ -244,7 +252,7 @@
             pltpu.VMEM((share, cols), F32),
             pltpu.SMEM((rows, slots), jnp.int32),
             pltpu.SMEM((rows, slots), jnp.int32),
-            dma, dma,
+            dma, dma, dma, dma, dma,
             dma((n,)), dma((n,)), dma((n,)), dma((n,)),
             dma((n,)), dma((n,)), dma((n,)), dma((n,)),
         ],
@@ -252,7 +260,7 @@
             collective_id=0, has_side_effects=True, vmem_limit_bytes=52 * 1024 * 1024
         ),
         name="product_and_gram",
-    )(a_blocks, own_blocks, pattern, pattern)
+    )(a_blocks, own_blocks, pattern)
 
 
 def lanes(x, width):

time: 55.3 us -> 51.3 us (0.928)
  Pallas kernels: 52.8 us -> 48.7 us
    pallas_call x1, Pallas kernels: 47.2 us -> 43.2 us  [product_and_gram(): pl.pallas_call(functools.partial(product_kernel, n, m), out_shape=(jax.Sh...]
where the time goes in v3:
time: 51.3 us; the launch traced here: 51.1 us
  Pallas kernels  48.7 us (95%)
  local copies, waits for them, and re-layouts  1.72 us (3%)
  between operations  0.65 us (1%)
    pallas_call x1, Pallas kernels, product_and_gram(): pl.pallas_call(functools.partial(product_kernel, n, m), out_shape=(jax.Sh...  43.2 us
    pallas_call x1, Pallas kernels, factor_and_basis(): pl.pallas_call(functools.partial(factor_kernel, 1.0 / nodes, STEP), out_s...  5.56 us
    unnamed x4, local copies, waits for them, and re-layouts  1.72 us

profile of v3, /device:TPU:0, one launch (start us, length us, event | category | flops | bytes accessed | tf_op | source)
XLA Modules:
  0.0 51.1 jit_solution(7453465496098836070)
XLA Ops:
  0.6 0.0 copy-start
  0.6 1.0 %copy-done = bf16[2048,128]{1,0:T(8,128)(2,1)S(1)} copy-done((bf16[2048,128]{1,0:T(8,128)(2,1)S(1)}, bf16[2048,128]{1,0:T(8,128)(2,1)}, u32[]{:S(2)}) %copy-start) | copy-done | bytes 524312
  1.7 0.0 copy-start.1
  1.7 0.7 %copy-done.1 = s32[8,8]{1,0:T(8,128)S(1)} copy-done((s32[8,8]{1,0:T(8,128)S(1)}, s32[8,8]{1,0:T(8,128)}, u32[]{:S(2)}) %copy-start.1) | copy-done | bytes 280
  2.4 43.2 %product_and_gram.1 = (f32[8,256,128]{2,1,0:T(8,128)S(1)}, f32[128,128]{1,0:T(8,128)S(1)}) custom-call(bf16[8,8,256,256]{3,2,1,0:T(8,128)(2,1)} %a_hbm.1, bf16[8,256,128]{2,1,0:T(8,128)(2,1)S(1)} %bitcast.2, s32[8,8]{1,0:T(8,128)S(1)} %copy-done.1), custom_call_target="tpu_custom_call" | custom-call | tf_op jit(solution)/shard_map/product_and_gram/pallas_call | solution.py:228
  45.5 5.6 %factor_and_basis.1 = (f32[8,256,128]{2,1,0:T(8,128)}, f32[128,128]{1,0:T(8,128)}) custom-call(f32[128,128]{1,0:T(8,128)S(1)} %get-tuple-element.6.gram, f32[8,256,128]{2,1,0:T(8,128)S(1)} %get-tuple-element.7.image_hbm), custom_call_target="tpu_custom_call" | custom-call | tf_op jit(solution)/shard_map/factor_and_basis/pallas_call | solution.py:360
Async XLA Ops:
  0.6 1.0 %copy-start = (bf16[2048,128]{1,0:T(8,128)(2,1)S(1)}, bf16[2048,128]{1,0:T(8,128)(2,1)}, u32[]{:S(2)}) copy-start(bf16[2048,128]{1,0:T(8,128)(2,1)} %param.4) | copy-start | bytes 1572868
  1.7 0.7 %copy-start.1 = (s32[8,8]{1,0:T(8,128)S(1)}, s32[8,8]{1,0:T(8,128)}, u32[]{:S(2)}) copy-start(s32[8,8]{1,0:T(8,128)} %pat_hbm.1) | copy-start | bytes 772

commit v4 on v3

--- a/solution.py
+++ b/solution.py
@@ -161,6 +161,18 @@
                 part.at[pl.ds(t * share, share)], gram_in.at[me], rs_send.at[t], rs_recv.at[me], t
             ).start()
 
+    @pl.loop(0, n - 1, unroll=unroll)
+    def _(k):
+        target = (me + k + 1) % n
+        remote(
+            req_out.at[target], req_in.at[me], req_send.at[target], req_recv.at[me], target
+        ).wait_send()
+        remote(
+            out_buf.at[target], land.at[me], dat_send.at[target], dat_recv.at[me], target
+        ).wait_send()
+
+    image_copy.wait()
+
     @pl.when(me < m)
     def _():
         gram_in[me] = part[pl.ds(pl.multiple_of(me * share, share), share), :]
@@ -188,11 +200,16 @@
         @pl.when(t != me)
         def _():
             remote(
+                part.at[pl.ds(t * share, share)], gram_in.at[me], rs_send.at[t], rs_recv.at[me], t
+            ).wait_send()
+
+    @pl.loop(0, m, unroll=unroll)
+    def _(t):
+        @pl.when(t != me)
+        def _():
+            remote(
                 chunk, gram_out.at[pl.ds(t * share, share)], ag_send.at[t], ag_recv.at[t], t
             ).wait_recv()
-            remote(
-                part.at[pl.ds(t * share, share)], gram_in.at[me], rs_send.at[t], rs_recv.at[me], t
-            ).wait_send()
 
     @pl.when(me < m)
     def _():
@@ -202,18 +219,6 @@
             remote(
                 chunk, gram_out.at[pl.ds(me * share, share)], ag_send.at[target], ag_recv.at[me], target
             ).wait_send()
-
-    @pl.loop(0, n - 1, unroll=unroll)
-    def _(k):
-        target = (me + k + 1) % n
-        remote(
-            req_out.at[target], req_in.at[me], req_send.at[target], req_recv.at[me], target
-        ).wait_send()
-        remote(
-            out_buf.at[target], land.at[me], dat_send.at[target], dat_recv.at[me], target
-        ).wait_send()
-
-    image_copy.wait()
 
 
 def product_and_gram(a_blocks, own_blocks, pattern):
@@ -236,7 +241,7 @@
             pl.BlockSpec(memory_space=pltpu.HBM),
             pl.BlockSpec(memory_space=pltpu.HBM),
         ],
-        out_specs=(pl.BlockSpec(memory_space=pl.ANY), vmem),
+        out_specs=(pl.BlockSpec(memory_space=pltpu.HBM), vmem),
         scratch_shapes=[
             pltpu.VMEM((rows, slots), jnp.int32),
             pltpu.SMEM((rows, slots), jnp.int32),
@@ -257,7 +262,7 @@
             dma((n,)), dma((n,)), dma((n,)), dma((n,)),
         ],
         compiler_params=pltpu.CompilerParams(
-            collective_id=0, has_side_effects=True, vmem_limit_bytes=52 * 1024 * 1024
+            collective_id=0, has_side_effects=True, vmem_limit_bytes=64 * 1024 * 1024
         ),
         name="product_and_gram",
     )(a_blocks, own_blocks, pattern)
@@ -278,11 +283,16 @@
     return high, middle, rest - middle
 
 
-def factor_kernel(scale, step, gram, image_hbm, basis_hbm, factor, image, result, in_sem, out_sem):
+def factor_kernel(
+    scale, step, gram_hbm, image_hbm, basis_hbm, factor, gram, image, result, gram_sem, in_sem, out_sem
+):
     cols = gram.shape[0]
     chunks, size, unused = image.shape
+    gram_copy = pltpu.make_async_copy(gram_hbm, gram, gram_sem)
+    gram_copy.start()
     image_copy = pltpu.make_async_copy(image_hbm, image, in_sem)
     image_copy.start()
+    gram_copy.wait()
     down = lax.broadcasted_iota(jnp.int32, (cols, cols), 0)
     across = lax.broadcasted_iota(jnp.int32, (cols, cols), 1)
     rest = jnp.concatenate([gram[...] * scale, jnp.where(down == across, 1.0, 0.0)], axis=1)
@@ -363,12 +373,13 @@
             jax.ShapeDtypeStruct(image.shape, F32),
             jax.ShapeDtypeStruct(gram.shape, F32),
         ),
-        in_specs=[vmem, pl.BlockSpec(memory_space=pl.ANY)],
-        out_specs=(pl.BlockSpec(memory_space=pl.ANY), vmem),
+        in_specs=[pl.BlockSpec(memory_space=pltpu.HBM)] * 2,
+        out_specs=(pl.BlockSpec(memory_space=pltpu.HBM), vmem),
         scratch_shapes=[
-            pltpu.VMEM(image.shape, F32), pltpu.VMEM(image.shape, F32), dma, dma((image.shape[0],)),
+            pltpu.VMEM(gram.shape, F32), pltpu.VMEM(image.shape, F32), pltpu.VMEM(image.shape, F32),
+            dma, dma, dma((image.shape[0],)),
         ],
-        compiler_params=pltpu.CompilerParams(vmem_limit_bytes=32 * 1024 * 1024),
+        compiler_params=pltpu.CompilerParams(vmem_limit_bytes=64 * 1024 * 1024),
         name="factor_and_basis",
     )(gram, image)
 

time: 51.3 us -> 50.8 us (level)
  local copies, waits for them, and re-layouts: 1.72 us -> 0 us
  Pallas kernels: 48.7 us -> 50 us
    unnamed x4 -> x0, local copies, waits for them, and re-layouts: 1.72 us -> none
    pallas_call x1, Pallas kernels: 5.56 us -> 6.34 us  [factor_and_basis(): pl.pallas_call(functools.partial(factor_kernel, 1.0 / nodes, STEP), out_s...]
where the time goes in v4:
time: 50.8 us; the launch traced here: 50.6 us
  Pallas kernels  50 us (98%)
  between operations  0.64 us (1%)
    pallas_call x1, Pallas kernels, product_and_gram(): pl.pallas_call(functools.partial(product_kernel, n, m), out_shape=(jax.Sh...  43.6 us
    pallas_call x1, Pallas kernels, factor_and_basis(): pl.pallas_call(functools.partial(factor_kernel, 1.0 / nodes, STEP), out_s...  6.34 us

profile of v4, /device:TPU:0, one launch (start us, length us, event | category | flops | bytes accessed | tf_op | source)
XLA Modules:
  0.0 50.6 jit_solution(3951107057532009760)
XLA Ops:
  0.6 43.6 %product_and_gram.1 = (f32[8,256,128]{2,1,0:T(8,128)}, f32[128,128]{1,0:T(8,128)}) custom-call(bf16[8,8,256,256]{3,2,1,0:T(8,128)(2,1)} %a_hbm.1, bf16[8,256,128]{2,1,0:T(8,128)(2,1)} %bitcast.2, s32[8,8]{1,0:T(8,128)} %pat_hbm.1), custom_call_target="tpu_custom_call" | custom-call | tf_op jit(solution)/shard_map/product_and_gram/pallas_call | solution.py:233
  44.3 6.3 %factor_and_basis.1 = (f32[8,256,128]{2,1,0:T(8,128)}, f32[128,128]{1,0:T(8,128)}) custom-call(f32[128,128]{1,0:T(8,128)} %get-tuple-element.6.gram_hbm, f32[8,256,128]{2,1,0:T(8,128)} %get-tuple-element.7.image_hbm), custom_call_target="tpu_custom_call" | custom-call | tf_op jit(solution)/shard_map/factor_and_basis/pallas_call | solution.py:370

commit v5 on v4

--- a/solution.py
+++ b/solution.py
@@ -130,14 +130,17 @@
 
     a_copy.wait()
 
-    for k in range(slots):
+    for k in range(1, slots, 2):
+        arrive(n - 2 - slots + k)
         arrive(n - 1 - slots + k)
 
         for r in range(rows):
             term = jnp.dot(
+                a_vm[r, slot_s[r, k - 1]], stage[index_s[r, k - 1]], preferred_element_type=F32
+            ) + jnp.dot(
                 a_vm[r, slot_s[r, k]], stage[index_s[r, k]], preferred_element_type=F32
             )
-            if k > 0:
+            if k > 1:
                 term = term + acc[r]
             acc[r] = term
             if k == slots - 1:
@@ -227,7 +230,7 @@
     cols = own_blocks.shape[2]
     share = 8
     m = cols // share
-    assert n >= m and n > slots and n & (n - 1) == 0
+    assert n >= m and n > slots and n & (n - 1) == 0 and slots % 2 == 0
     vmem = pl.BlockSpec(memory_space=pltpu.VMEM)
     dma = pltpu.SemaphoreType.DMA
     return pl.pallas_call(

time: 50.8 us -> 51.3 us (level)
  no operation moved by 1% of the time
where the time goes in v5:
time: 51.3 us; the launch traced here: 51.1 us
  Pallas kernels  50.4 us (98%)
  between operations  0.64 us (1%)
    pallas_call x1, Pallas kernels, product_and_gram(): pl.pallas_call(functools.partial(product_kernel, n, m), out_shape=(jax.Sh...  44.1 us
    pallas_call x1, Pallas kernels, factor_and_basis(): pl.pallas_call(functools.partial(factor_kernel, 1.0 / nodes, STEP), out_s...  6.35 us

profile of v5, /device:TPU:0, one launch (start us, length us, event | category | flops | bytes accessed | tf_op | source)
XLA Modules:
  0.0 51.1 jit_solution(6175243349720266690)
XLA Ops:
  0.6 44.1 %product_and_gram.1 = (f32[8,256,128]{2,1,0:T(8,128)}, f32[128,128]{1,0:T(8,128)}) custom-call(bf16[8,8,256,256]{3,2,1,0:T(8,128)(2,1)} %a_hbm.1, bf16[8,256,128]{2,1,0:T(8,128)(2,1)} %bitcast.2, s32[8,8]{1,0:T(8,128)} %pat_hbm.1), custom_call_target="tpu_custom_call" | custom-call | tf_op jit(solution)/shard_map/product_and_gram/pallas_call | solution.py:236
  44.7 6.3 %factor_and_basis.1 = (f32[8,256,128]{2,1,0:T(8,128)}, f32[128,128]{1,0:T(8,128)}) custom-call(f32[128,128]{1,0:T(8,128)} %get-tuple-element.6.gram_hbm, f32[8,256,128]{2,1,0:T(8,128)} %get-tuple-element.7.image_hbm), custom_call_target="tpu_custom_call" | custom-call | tf_op jit(solution)/shard_map/factor_and_basis/pallas_call | solution.py:373
